TPU v7x, 128 devices: a whole 4x4x4 slice. The times are simulated.
128 devices in a mesh: outer: 4 (over z_lo, core), fsdp: 32 (over y, z_hi, x).
Axes of the slice: x: 4, y: 4, z: 4 (z_hi: 2, z_lo: 2; z = z_hi * 2 + z_lo), core: 2. Of those that a mesh axis runs over, the one named last changes fastest.
Arguments:
- partials: bfloat16 [128, 32768, 128], P(('outer', 'fsdp')), may hold values from -4 to 4
- worker_residual: float32 [4, 32768, 128], P('outer', 'fsdp'), may hold values from -4 to 4
- server_residual: float32 [32, 1024, 128], P('fsdp', 'outer'), may hold values from -4 to 4
- master: float32 [32, 1024, 128], P('fsdp', 'outer'), may hold values from -0.3 to 0.3
- first_moment: float32 [32, 1024, 128], P('fsdp', 'outer'), may hold values from -6 to 6
- second_moment: float32 [32, 1024, 128], P('fsdp', 'outer'), may hold values from 0.5 to 50
Outputs:
- new_master: float32 [32, 1024, 128], P('fsdp', 'outer')
- new_first: float32 [32, 1024, 128], P('fsdp', 'outer')
- new_second: float32 [32, 1024, 128], P('fsdp', 'outer')
- params_full: bfloat16 [32768, 128], replicated
All inputs are finite; a program needn't handle non-finite values. Where the computation divides by a largest or mean magnitude, that divisor is 1e-20 or more.
Results may differ from a plain program's by a relative error of at most 0.0035.
Values may be sent and summed in bfloat16 or wider, within the bound.
A program may use at most 128 MiB of HBM per device.

v0:
```python
import jax
import jax.numpy as jnp
from jax import lax
from jax.sharding import PartitionSpec as P

STEP = 10


def local(partials, worker_residual, server_residual, master, first_moment, second_moment):
    local_grad = partials[0]
    pod_grad = lax.psum_scatter(
        local_grad.astype(jnp.float32), "fsdp", scatter_dimension=0, tiled=True
    )
    worker = pod_grad + worker_residual[0]
    worker_scale = jnp.max(jnp.abs(worker), axis=-1) + 1e-06
    coded = (worker / worker_scale[:, None]).astype(jnp.bfloat16)
    got_codes, got_scales = (
        lax.all_to_all(coded[None], "outer", split_axis=1, concat_axis=0, tiled=True),
        lax.all_to_all(
            worker_scale[None].astype(jnp.bfloat16),
            "outer",
            split_axis=1,
            concat_axis=0,
            tiled=True,
        ).astype(jnp.float32),
    )
    total = jnp.sum(got_codes.astype(jnp.float32) * got_scales[:, :, None], axis=0)
    server = total + server_residual[0]
    server_scale = jnp.max(jnp.abs(server), axis=-1) + 1e-06
    server_code = (server / server_scale[:, None]).astype(jnp.bfloat16)
    grad = server_code.astype(jnp.float32) * server_scale[:, None]
    new_first = 0.9 * first_moment[0] + 0.1 * grad
    new_second = 0.95 * second_moment[0] + 0.05 * grad * grad
    first_hat = new_first / (1.0 - 0.9**STEP)
    second_hat = new_second / (1.0 - 0.95**STEP)
    old_master = master[0]
    new_master = old_master - 0.01 * (first_hat / (jnp.sqrt(second_hat) + 1e-08) + 0.1 * old_master)
    weights = new_master.astype(jnp.bfloat16)
    pod_params = lax.all_gather(weights, "outer", axis=0, tiled=True)
    params_full = lax.all_gather(pod_params, "fsdp", axis=0, tiled=True)
    return (new_master[None], new_first[None], new_second[None], params_full)


def solution(mesh):
    placed = (
        P(("outer", "fsdp"), None, None),
        P("outer", "fsdp", None),
        P("fsdp", "outer", None),
        P("fsdp", "outer", None),
        P("fsdp", "outer", None),
        P("fsdp", "outer", None),
    )
    return jax.shard_map(
        local,
        mesh=mesh,
        in_specs=placed,
        out_specs=(
            P("fsdp", "outer", None),
            P("fsdp", "outer", None),
            P("fsdp", "outer", None),
            P(),
        ),
        check_vma=False,
    )
```

profile of v0, /device:TPU:1, one launch (start us, length us, event | category | flops | bytes accessed | tf_op | source)
XLA Modules:
  0.0 388.6 jit_solution(14105053025133535130)
XLA Ops:
  7.2 0.0 reduce-scatter.2.cloned.1.call-start
  7.2 9.5 %bitcast_convert_fusion = f32[32768,128]{1,0:T(8,128)} fusion(bf16[1,32768,128]{2,1,0:T(8,128)(2,1)} %param.6), kind=kLoop, calls=%fused_computation | loop fusion | flops 4194304 | bytes 25165824 | tf_op jit(solution)/shard_map/convert_element_type | solution.py:12
  16.7 0.0 copy-start
  16.7 0.0 copy-start.1
  16.7 0.0 copy-start.2
  16.7 0.0 copy-start.3
  16.7 0.0 copy-start.4
  16.7 0.0 reduce-scatter.2.cloned.1.call-update
  16.7 208.6 %reduce-scatter.2.cloned.1.call-done = f32[1024,128]{1,0:T(8,128)} async-done(((f32[32768,128]{1,0:T(8,128)}), f32[1024,128]{1,0:T(8,128)}) %reduce-scatter.2.cloned.1.call-update) | async-done | bytes 524304 | tf_op jit(solution)/shard_map/reduce_scatter | solution.py:11
  225.4 0.0 copy-done
  225.4 1.3 abs_reduce_fusion
  226.7 0.5 broadcast.69
  227.2 0.7 reduce.1
  227.8 0.6 reshape.109
  228.4 23.4 %all-to-all-start.1 = ((bf16[4,2,128]{2,1,0:T(2,128)(2,1)}), bf16[4,2,128]{2,1,0:T(2,128)(2,1)S(1)}, u32[]{:S(2)}, u32[]{:S(2)}) async-start(bf16[4,2,128]{2,1,0:T(2,128)(2,1)} %reshape.109), calls=%async_computation.2 | async-start | bytes 4096 | tf_op jit(solution)/shard_map/all_to_all | solution.py:19
  251.8 1.2 fusion
  253.0 0.4 copy.16
  253.5 2.2 reduce
  255.7 0.8 reshape.107
  256.4 0.0 all-to-all-done.1
  256.5 3.4 all-to-all-start
  259.9 0.0 all-gather.2.cloned.1.call-start
  259.9 5.1 %all-to-all-done = bf16[4,2,16384]{2,1,0:T(2,128)(2,1)S(1)} async-done(((bf16[4,2,16384]{2,1,0:T(2,128)(2,1)}), bf16[4,2,16384]{2,1,0:T(2,128)(2,1)S(1)}, u32[]{:S(2)}, u32[]{:S(2)}) %all-to-all-start) | async-done | bytes 262176 | tf_op jit(solution)/shard_map/all_to_all | solution.py:18
  265.0 0.3 reshape.108
  265.3 0.5 bitcast_convert_fusion.1
  265.9 0.2 multiply_reduce_fusion
  266.1 0.0 copy-done.1
  266.1 0.1 abs_reduce_fusion.1
  266.2 0.0 copy-done.2
  266.2 0.0 copy-done.3
  266.2 0.0 copy-done.4
  266.2 0.2 fusion.9
  266.4 6.9 %all_gather.6 = bf16[1024,128]{1,0:T(8,128)(2,1)} all-gather(bf16[256,128]{1,0:T(8,128)(2,1)S(1)} %fusion.9), channel_id=1, replica_groups=mesh['outer'=4,'fsdp'=32] {'outer'}, dimensions={0}, use_global_device_ids=true | all-gather | bytes 327680 | tf_op jit(solution)/shard_map/all_gather | solution.py:39
  273.4 0.0 all-gather.2.cloned.1.call-update
  273.4 0.9 multiply_subtract_fusion
  274.3 100.4 %all-gather.2.cloned.1.call-done = bf16[32768,128]{1,0:T(8,128)(2,1)} async-done(((bf16[1024,128]{1,0:T(8,128)(2,1)}), bf16[32768,128]{1,0:T(8,128)(2,1)}) %all-gather.2.cloned.1.call-update) | async-done | bytes 8388624 | tf_op jit(solution)/shard_map/all_gather | solution.py:40
  374.7 7.1 %copy.18 = bf16[32768,128]{1,0:T(8,128)(2,1)} copy(bf16[32768,128]{1,0:T(8,128)(2,1)} %all-gather.2.cloned.1.call-done) | data formatting | bytes 16777216
  (6 shorter events, 0.0 us)
Async XLA Ops:
  7.2 218.2 %reduce-scatter.2.cloned.1.call-start = ((), (), s32[]{:S(2)}) async-start(), calls=%async_computation.3 | async-start | bytes 17301504 | tf_op jit(solution)/shard_map/reduce_scatter | solution.py:11
  16.7 208.7 %copy-start = (f32[1,1024,128]{2,1,0:T(8,128)S(1)}, f32[1,1024,128]{2,1,0:T(8,128)}, u32[]{:S(2)}) copy-start(f32[1,1024,128]{2,1,0:T(8,128)} %param.7) | copy-start | bytes 1572868
  16.7 249.4 %copy-start.1 = (f32[1,256,128]{2,1,0:T(8,128)S(1)}, f32[1,256,128]{2,1,0:T(8,128)}, u32[]{:S(2)}) copy-start(f32[1,256,128]{2,1,0:T(8,128)} %param.8) | copy-start | bytes 393220
  16.7 249.5 %copy-start.2 = (f32[1,256,128]{2,1,0:T(8,128)S(1)}, f32[1,256,128]{2,1,0:T(8,128)}, u32[]{:S(2)}) copy-start(f32[1,256,128]{2,1,0:T(8,128)} %param.9) | copy-start | bytes 393220
  16.7 249.5 %copy-start.3 = (f32[1,256,128]{2,1,0:T(8,128)S(1)}, f32[1,256,128]{2,1,0:T(8,128)}, u32[]{:S(2)}) copy-start(f32[1,256,128]{2,1,0:T(8,128)} %param.10) | copy-start | bytes 393220
  16.7 249.5 %copy-start.4 = (f32[1,256,128]{2,1,0:T(8,128)S(1)}, f32[1,256,128]{2,1,0:T(8,128)}, u32[]{:S(2)}) copy-start(f32[1,256,128]{2,1,0:T(8,128)} %param.11) | copy-start | bytes 393220
  228.4 28.0 %all-to-all-start.1 = ((bf16[4,2,128]{2,1,0:T(2,128)(2,1)}), bf16[4,2,128]{2,1,0:T(2,128)(2,1)S(1)}, u32[]{:S(2)}, u32[]{:S(2)}) async-start(bf16[4,2,128]{2,1,0:T(2,128)(2,1)} %reshape.109), calls=%async_computation.2 | async-start | bytes 4096 | tf_op jit(solution)/shard_map/all_to_all | solution.py:19
  256.5 8.6 %all-to-all-start = ((bf16[4,2,16384]{2,1,0:T(2,128)(2,1)}), bf16[4,2,16384]{2,1,0:T(2,128)(2,1)S(1)}, u32[]{:S(2)}, u32[]{:S(2)}) async-start(bf16[4,2,16384]{2,1,0:T(2,128)(2,1)} %reshape.107), calls=%async_computation.1 | async-start | bytes 524288 | tf_op jit(solution)/shard_map/all_to_all | solution.py:18
  259.9 114.8 %all-gather.2.cloned.1.call-start = ((), (), s32[]{:S(2)}) async-start(), calls=%async_computation.4 | async-start | bytes 8650752 | tf_op jit(solution)/shard_map/all_gather | solution.py:40
Sparse Core Ops, SparseCore 0:
  16.9 208.4 reduce-scatter.1
  273.5 101.1 all-gather.1
where the time goes:
time: 389 us
  waiting for transfers between devices  314 us (81%)
  starting transfers between devices  26.9 us (7%)
  other arithmetic  16.8 us (4%)
  between operations  14.2 us (4%)
  local copies, waits for them, and re-layouts  9.69 us (2%)
  blocking collectives  6.94 us (2%)
    reduce_scatter x1, waiting for transfers between devices, local(): lax.psum_scatter(local_grad.astype(jnp.float32), 'fsdp', scatter_dimensio...  209 us
    all_gather x1, waiting for transfers between devices, local(): params_full = lax.all_gather(pod_params, 'fsdp', axis=0, tiled=True)  100 us
    all_to_all x1, starting transfers between devices, local(): lax.all_to_all(worker_scale[None].astype(jnp.bfloat16), 'outer', split_ax...  23.4 us
    convert_element_type x1, other arithmetic, local(): local_grad.astype(jnp.float32)  9.47 us
    unnamed x17, local copies, waits for them, and re-layouts  9.27 us
  transfers between devices with their start and end apart: 4, of which 3 were waited for; matrix products, arithmetic and copies ran while one was open for 1% of the time, Pallas kernels for 0%

commit v1 on v0

v1 whole, which is shorter than its diff:
```python
import functools

import jax
import jax.numpy as jnp
from jax import lax
from jax.experimental import pallas as pl
from jax.experimental.pallas import tpu as pltpu
from jax.sharding import PartitionSpec as P

STEP = 10
MESH = pl.DeviceIdType.MESH
BF, F32 = jnp.bfloat16, jnp.float32
NX, NY, NH, NL, NC = 4, 4, 2, 2, 2
ROWS = 256

GROUPS = (64, 64, 64, 64)
EARLY = (("xyz", 0, 32), ("yxz", 32, 32))
LATE = (("xyz", 0, 16), ("yzx", 16, 16), ("zxy", 32, 16), ("yxz", 48, 16))
PARTS = (EARLY, EARLY, EARLY, LATE)
RELATIVE = [(b, h) for b in range(4) for h in range(2) if (b, h) != (0, 0)]


class At:
    def __init__(self):
        o, f = lax.axis_index("outer"), lax.axis_index("fsdp")
        self.o, self.f = o, f
        self.zl, self.c = o // 2, o % 2
        self.y, self.zh, self.x = f // 8, (f // 4) % 2, f % 4
        self.z = self.zh * 2 + self.zl

    def device(self, x=0, y=0, z=0, c=0):
        z = (self.z + z) % 4
        return {
            "outer": (z % 2) * 2 + (self.c + c) % 2,
            "fsdp": ((self.y + y) % 4) * 8 + (z // 2) * 4 + (self.x + x) % 4,
        }

    def pod(self, j):
        return (self.zl + j // 2) % 2, (self.c + j % 2) % 2


def partners():
    found = set()
    for b in range(1, 4):
        found |= {(b, 0, 0, 0), (0, b, 0, 0)}
    for b, h in RELATIVE:
        found |= {(b, 0, 2 * h, 0), (0, b, 2 * h, 0)}
    found |= {(0, 0, 1, 0), (0, 0, 3, 0), (0, 0, 2, 0), (0, 0, 0, 1)}
    return sorted(found)


class Copies:
    def __init__(self, send, recv):
        self.send, self.recv, self.n, self.started = send, recv, 0, []

    def __call__(self, src, dst, to):
        copy = pltpu.make_async_remote_copy(
            src_ref=src, dst_ref=dst, send_sem=self.send.at[self.n], recv_sem=self.recv.at[self.n],
            device_id=to, device_id_type=MESH,
        )
        self.n += 1
        copy.start()
        self.started.append(copy)
        return copy


def kernel(parts_hbm, wres_hbm, sres_hbm, mast_hbm, mom1_hbm, mom2_hbm, new_mast, new_first, new_second, full,
           grads, wres, own, got_a, sum32, sum16, got_b, deq, got_o, load_sem, send_sem, recv_sem):
    at = At()
    starts = [sum(GROUPS[:g]) for g in range(len(GROUPS))]
    rows = [pl.ds(s, r) for s, r in zip(starts, GROUPS)]
    n_groups = len(GROUPS)

    loads = []
    for g in range(n_groups):
        view = (slice(None),) * 4 + (rows[g],)
        loads.append(pltpu.make_async_copy(parts_hbm.at[view], grads.at[view], load_sem.at[g]))
    small = [
        pltpu.make_async_copy(src, dst, load_sem.at[n_groups + i])
        for i, (src, dst) in enumerate(
            [(wres_hbm, wres), (sres_hbm, own.at[0]), (mast_hbm, own.at[1]), (mom1_hbm, own.at[2]), (mom2_hbm, own.at[3])]
        )
    ]
    for copy in loads + small:
        copy.start()

    barrier = pltpu.get_barrier_semaphore()
    met = partners()
    for x, y, z, c in met:
        pl.semaphore_signal(barrier, inc=1, device_id=at.device(x, y, z, c), device_id_type=MESH)
    zl, c = at.pod(3)
    pl.semaphore_signal(barrier, inc=1, device_id={"outer": zl * 2 + c, "fsdp": at.f}, device_id_type=MESH)
    pl.semaphore_wait(barrier, len(met) + 1)

    send = Copies(send_sem, recv_sem)
    mine = (at.x, at.y)
    a, b, d, outs = {}, {}, {}, {}

    def chunk(g, s, to, h):
        if s == 0:
            return grads.at[:, h, to, 0:2, rows[g], :]
        return grads.at[to, h, :, 2:4, rows[g], :]

    def along(s, n):
        return at.device(x=n) if s == 0 else at.device(y=n)

    def a1(g):
        loads[g].wait()
        for s in range(2):
            i = mine[s]
            ahead, behind, across = (i + 1) % 4, (i + 3) % 4, (i + 2) % 4
            into = lambda k: got_a.at[s, k, :, :, rows[g], :]
            a[g, s] = [
                send(chunk(g, s, across, 0), into(0), along(s, 1)),
                send(chunk(g, s, across, 1), into(1), along(s, 3)),
                send(chunk(g, s, ahead, 1), into(2), along(s, 1)),
                send(chunk(g, s, behind, 0), into(3), along(s, 3)),
            ]

    def a2(g):
        for s in range(2):
            i = mine[s]
            into = lambda k: got_a.at[s, k, :, :, rows[g], :]
            for k, to, n in ((0, (i + 1) % 4, 1), (1, (i + 3) % 4, 3)):
                a[g, s][k].wait_recv()
                block = chunk(g, s, to, k)
                block[...] = (block[...].astype(F32) + into(k)[...].astype(F32)).astype(BF)
                a[g, s].append(send(block, into(4 + k), along(s, n)))

    def a3(g):
        for s in range(2):
            i, j = mine[s], mine[1 - s]
            into = lambda k: got_a.at[s, k, :, :, rows[g], :]
            for h, (k, m) in enumerate(((4, 3), (2, 5))):
                a[g, s][k].wait_recv()
                a[g, s][m].wait_recv()
                summed = chunk(g, s, i, h)[...].astype(F32) + into(k)[...].astype(F32) + into(m)[...].astype(F32)
                sum32[s, :, h, :, 0:GROUPS[g], :] = summed
                sum16[s, :, h, :, rows[g], :] = summed.astype(BF)
            b[g, s] = []
            for n, (db, dh) in enumerate(RELATIVE):
                to = along(1 - s, db) if dh == 0 else (at.device(y=db, z=2) if s == 0 else at.device(x=db, z=2))
                b[g, s].append(
                    send(sum16.at[s, (j + db) % 4, (at.zh + dh) % 2, :, rows[g], :], got_b.at[s, n, :, rows[g], :], to)
                )
            own_sum = sum32[s, j, at.zh, :, 0:GROUPS[g], :]
            deq[2 * s:2 * s + 2, rows[g], :] = own_sum

    def b1(g):
        for s in range(2):
            both = slice(2 * s, 2 * s + 2)
            pod_grad = deq[both, rows[g], :]
            for n, copy in enumerate(b[g, s]):
                copy.wait_recv()
                pod_grad = pod_grad + got_b[s, n, :, rows[g], :].astype(F32)
            worker = pod_grad + wres[both, rows[g], :]
            scale = jnp.max(jnp.abs(worker), axis=-1, keepdims=True) + 1e-06
            coded = (worker / scale).astype(BF)
            deq[both, rows[g], :] = coded.astype(F32) * scale
        d[g] = []
        for j in range(1, 4):
            zl, c = at.pod(j)
            d[g].append(send(deq.at[zl * 2 + c, rows[g], :], got_o.at[j - 1, rows[g], :], {"outer": zl * 2 + c, "fsdp": at.f}))

    def c1(g):
        total = deq[at.o, rows[g], :]
        for j in range(3):
            d[g][j].wait_recv()
            total = total + got_o[j, rows[g], :]
        server = total + own[0, rows[g], :]
        scale = jnp.max(jnp.abs(server), axis=-1, keepdims=True) + 1e-06
        code = (server / scale).astype(BF)
        grad = code.astype(F32) * scale
        first = 0.9 * own[2, rows[g], :] + 0.1 * grad
        second = 0.95 * own[3, rows[g], :] + 0.05 * grad * grad
        first_hat = first / (1.0 - 0.9**STEP)
        second_hat = second / (1.0 - 0.95**STEP)
        old = own[1, rows[g], :]
        new = old - 0.01 * (first_hat / (jnp.sqrt(second_hat) + 1e-08) + 0.1 * old)
        new_mast[rows[g], :] = new
        new_first[rows[g], :] = first
        new_second[rows[g], :] = second
        full[at.y, at.zh, at.x, at.zl, at.c, rows[g], :] = new.astype(BF)
        for p in range(len(PARTS[g])):
            gather_one(g, p, 0)

    def region(g, p, spread, halves=None):
        order, first, count = PARTS[g][p]
        pick = {"x": at.x, "y": at.y}
        for axis in spread:
            pick[axis] = slice(None)
        zh, zl = (slice(None), slice(None)) if "z" in spread else (at.zh, at.zl)
        if halves is not None:
            axis, offset, lead, half = halves
            if axis == "z":
                z = (at.z + offset) % 4
                zh, zl = z // 2, z % 2
            else:
                pick[axis] = ((at.x if axis == "x" else at.y) + offset) % 4
            if half is not None:
                if lead == "z":
                    zh = slice(half, half + 1)
                else:
                    pick[lead] = slice(2 * half, 2 * half + 2)
        return full.at[pick["y"], zh, pick["x"], zl, at.c, pl.ds(starts[g] + first, count), :]

    def to_axis(axis, n):
        return at.device(**{axis: n})

    sibling = at.device(c=1)
    cores = []

    def gather_one(g, p, stage):
        order = PARTS[g][p][0]
        key = (g, p)
        if stage > 0:
            for copy in outs[key]:
                copy.wait_recv()
        if stage < 2:
            piece = region(g, p, order[:stage])
            outs[key] = [send(piece, piece, to_axis(order[stage], n)) for n in (1, 3, 2)]
        elif stage == 2:
            piece = region(g, p, order[:2])
            outs[key] = [send(piece, piece, to_axis(order[2], n)) for n in (1, 3)]
            cores.append(send(piece, piece, sibling))
        elif stage == 3:
            back = region(g, p, order[:2], (order[2], 3, order[0], 0))
            front = region(g, p, order[:2], (order[2], 1, order[0], 1))
            outs[key] = [send(back, back, to_axis(order[2], 1)), send(front, front, to_axis(order[2], 3))]
            for n in (1, 3):
                piece = region(g, p, order[:2], (order[2], n, None, None))
                cores.append(send(piece, piece, sibling))
        else:
            piece = region(g, p, order[:2], (order[2], 2, None, None))
            cores.append(send(piece, piece, sibling))

    def gather(g, stage):
        for p in range(len(PARTS[g])):
            gather_one(g, p, stage)

    for copy in small:
        copy.wait()
    a1(0)
    for t in range(n_groups + 4):
        if t < n_groups:
            a2(t)
        if t + 1 < n_groups:
            a1(t + 1)
        if 0 <= t - 2 < n_groups:
            gather(t - 2, 1)
        if 0 <= t - 3 < n_groups:
            gather(t - 3, 3)
        if 0 <= t - 1 < n_groups:
            b1(t - 1)
        if 0 <= t - 2 < n_groups:
            gather(t - 2, 2)
        if t < n_groups:
            a3(t)
        if 0 <= t - 1 < n_groups:
            c1(t - 1)
        if 0 <= t - 3 < n_groups:
            gather(t - 3, 4)
    for copy in cores:
        copy.wait_recv()
    for copy in send.started:
        copy.wait_send()


def copies_needed():
    per_group = 2 * (6 + 7) + 3
    return len(GROUPS) * per_group + sum(len(p) for p in PARTS) * (3 + 3 + 2 + 1 + 2 + 2 + 1)


def local(partials, worker_residual, server_residual, master, first_moment, second_moment):
    grads = partials.reshape(NY, NH, NX, NL * NC, ROWS, 128)
    wres = worker_residual.reshape(NL * NC, ROWS, 128)
    flat = [v.reshape(ROWS, 128) for v in (server_residual, master, first_moment, second_moment)]
    n = copies_needed()
    any_space = pl.BlockSpec(memory_space=pl.ANY)
    vmem = pl.BlockSpec(memory_space=pltpu.VMEM)
    tall = max(GROUPS)
    shard = jax.ShapeDtypeStruct((ROWS, 128), F32)
    new_mast, new_first, new_second, full = pl.pallas_call(
        kernel,
        out_shape=(shard, shard, shard, pltpu.VMEM((NY, NH, NX, NL, NC, ROWS, 128), BF)),
        in_specs=[any_space] * 6,
        out_specs=(vmem,) * 4,
        scratch_shapes=[
            pltpu.VMEM((NY, NH, NX, NL * NC, ROWS, 128), BF),
            pltpu.VMEM((NL * NC, ROWS, 128), F32),
            pltpu.VMEM((4, ROWS, 128), F32),
            pltpu.VMEM((2, 6, 4, 2, ROWS, 128), BF),
            pltpu.VMEM((2, 4, 2, 2, tall, 128), F32),
            pltpu.VMEM((2, 4, 2, 2, ROWS, 128), BF),
            pltpu.VMEM((2, 7, 2, ROWS, 128), BF),
            pltpu.VMEM((4, ROWS, 128), F32),
            pltpu.VMEM((3, ROWS, 128), F32),
            pltpu.SemaphoreType.DMA((len(GROUPS) + 5,)),
            pltpu.SemaphoreType.DMA((n,)),
            pltpu.SemaphoreType.DMA((n,)),
        ],
        compiler_params=pltpu.CompilerParams(collective_id=0, has_side_effects=True, vmem_limit_bytes=44 * 2**20),
    )(grads, wres, *flat)
    return new_mast[None], new_first[None], new_second[None], full.reshape(NY * NH * NX * NL * NC * ROWS, 128)


def solution(mesh):
    placed = (
        P(("outer", "fsdp"), None, None),
        P("outer", "fsdp", None),
        P("fsdp", "outer", None),
        P("fsdp", "outer", None),
        P("fsdp", "outer", None),
        P("fsdp", "outer", None),
    )
    return jax.shard_map(
        local,
        mesh=mesh,
        in_specs=placed,
        out_specs=(P("fsdp", "outer", None), P("fsdp", "outer", None), P("fsdp", "outer", None), P()),
        check_vma=False,
    )
```

time: 389 us -> 118 us (0.30)
  waiting for transfers between devices: 314 us -> 0 us
  Pallas kernels: 0 us -> 107 us
  starting transfers between devices: 26.9 us -> 0 us
  other arithmetic: 16.8 us -> 0 us
  between operations: 14.2 us -> 0.65 us
  blocking collectives: 6.94 us -> 0 us
    reduce_scatter x1 -> x0, waiting for transfers between devices: 209 us -> none  [local(): lax.psum_scatter(local_grad.astype(jnp.float32), 'fsdp', scatter_dimensio...]
    pallas_call x0 -> x1, Pallas kernels: none -> 107 us  [local(): pl.pallas_call(kernel, out_shape=(shard, shard, shard, pltpu.VMEM((NY, NH...]
    all_gather x1 -> x0, waiting for transfers between devices: 100 us -> none  [local(): params_full = lax.all_gather(pod_params, 'fsdp', axis=0, tiled=True)]
    all_to_all x2 -> x0, starting transfers between devices: 26.8 us -> none  [the longest x1 23.4 us: local(): lax.all_to_all(worker_scale[None].astype(jnp.bfloat16), 'outer', split_ax...]
    convert_element_type x5 -> x0, other arithmetic: 10.2 us -> none  [the longest x1 9.47 us: local(): local_grad.astype(jnp.float32)]
    all_gather x1 -> x0, blocking collectives: 6.94 us -> none  [local(): pod_params = lax.all_gather(weights, 'outer', axis=0, tiled=True)]
    all_to_all x2 -> x0, waiting for transfers between devices: 5.1 us -> none  [the longest x1 5.1 us: local(): lax.all_to_all(coded[None], 'outer', split_axis=1, concat_axis=0, tiled=T...]
    unnamed x17 -> x14, local copies, waits for them, and re-layouts: 9.27 us -> 10 us
  transfers between devices with their start and end apart: 4 -> 0, of which waited for: 3 -> 0; matrix products, arithmetic and copies ran while one was open for 1% -> 0% of each run, Pallas kernels for 0% -> 0%
where the time goes in v1:
time: 118 us; the launch traced here: 117 us
  Pallas kernels  107 us (91%)
  local copies, waits for them, and re-layouts  10 us (8%)
    pallas_call x1, Pallas kernels, local(): pl.pallas_call(kernel, out_shape=(shard, shard, shard, pltpu.VMEM((NY, NH...  107 us
    unnamed x14, local copies, waits for them, and re-layouts  10 us

profile of v1, /device:TPU:1, one launch (start us, length us, event | category | flops | bytes accessed | tf_op | source)
XLA Modules:
  0.0 117.5 jit_solution(3028471412672859275)
XLA Ops:
  0.6 0.0 copy-start
  0.6 1.0 copy-done
  1.7 0.0 copy-start.1
  1.7 0.9 copy-done.1
  2.6 0.0 copy-start.2
  2.6 0.9 copy-done.2
  3.5 0.0 copy-start.3
  3.5 0.9 copy-done.3
  4.4 0.0 copy-start.4
  4.4 0.9 copy-done.4
  5.3 106.8 %shard_map.93 = (f32[256,128]{1,0:T(8,128)S(1)}, f32[256,128]{1,0:T(8,128)S(1)}, f32[256,128]{1,0:T(8,128)S(1)}, bf16[4,2,4,2,2,256,128]{6,5,4,3,2,1,0:T(8,128)(2,1)S(1)}) custom-call(bf16[4,2,4,4,256,128]{5,4,3,2,1,0:T(8,128)(2,1)} %bitcast.19, f32[4,256,128]{2,1,0:T(8,128)S(1)} %bitcast.11, f32[256,128]{1,0:T(8,128)S(1)} %bitcast.12, ...), custom_call_target="tpu_custom_call" | custom-call | tf_op jit(solution)/shard_map/pallas_call | solution.py:283
  112.1 3.4 %copy.14 = bf16[32768,128]{1,0:T(8,128)(2,1)} copy(bf16[32768,128]{1,0:T(8,128)(2,1)S(1)} %bitcast.10) | data formatting | bytes 16777216
  115.5 0.7 copy.15
  116.1 0.7 copy.16
  116.8 0.7 copy.17
Async XLA Ops:
  0.6 1.0 copy-start
  1.7 0.9 copy-start.1
  2.6 0.9 copy-start.2
  3.5 0.9 copy-start.3
  4.4 0.9 copy-start.4

commit v2 on v1

v2 whole, which is shorter than its diff:
```python
import functools

import jax
import jax.numpy as jnp
from jax import lax
from jax.experimental import pallas as pl
from jax.experimental.pallas import tpu as pltpu
from jax.sharding import PartitionSpec as P

STEP = 10
MESH = pl.DeviceIdType.MESH
BF, F32 = jnp.bfloat16, jnp.float32
NX, NY, NH, NL, NC = 4, 4, 2, 2, 2
ROWS = 256

GROUPS = (("n", 64), ("n", 64), ("n", 64), ("z", 32), ("z", 32))
BATCHES = (
    ((0, 1, 2), (("xyz", 0, 64), ("yzx", 64, 64), ("zxy", 128, 64))),
    ((3, 4), (("xyz", 192, 16), ("yzx", 208, 16), ("zxy", 224, 32))),
)
TIMES = (
    {"a1": -9, "a2": 5.5, "a3": 12, "b": 18, "c": 24, "d": 29},
    {"a1": -8, "a2": 14, "a3": 21, "b": 27, "c": 33, "d": 38},
    {"a1": 7, "a2": 23, "a3": 30, "b": 36, "c": 42, "d": 47},
    {"z1": -7, "z2": 14, "a2": 20, "a3": 25, "b": 31, "d": 36},
    {"z1": -6, "z2": 24.5, "a2": 32, "a3": 37, "b": 41, "d": 45},
)
GATHER_TIMES = (
    {"g1": 51, "g2": 55, "g3": 60, "g4": 64},
    {"g1": 52, "g2": 56, "g3": 61, "g4": 65},
)


class At:
    def __init__(self):
        o, f = lax.axis_index("outer"), lax.axis_index("fsdp")
        self.o, self.f = o, f
        self.zl, self.c = o // 2, o % 2
        self.y, self.zh, self.x = f // 8, (f // 4) % 2, f % 4
        self.z = self.zh * 2 + self.zl

    def device(self, x=0, y=0, z=0, c=0):
        z = (self.z + z) % 4
        return {
            "outer": (z % 2) * 2 + (self.c + c) % 2,
            "fsdp": ((self.y + y) % 4) * 8 + (z // 2) * 4 + (self.x + x) % 4,
        }

    def pod(self, j):
        return (self.zl + j // 2) % 2, (self.c + j % 2) % 2


def partners():
    found = {(0, 0, 0, 1)}
    for b in range(1, 4):
        found |= {(b, 0, 0, 0), (0, b, 0, 0), (0, 0, b, 0)}
    return sorted(found)


class Copies:
    def __init__(self, send, recv):
        self.send, self.recv, self.n, self.started = send, recv, 0, []

    def __call__(self, src, dst, to):
        copy = pltpu.make_async_remote_copy(
            src_ref=src, dst_ref=dst, send_sem=self.send.at[self.n], recv_sem=self.recv.at[self.n],
            device_id=to, device_id_type=MESH,
        )
        self.n += 1
        copy.start()
        self.started.append(copy)
        return copy


def kernel(parts_hbm, wres_hbm, sres_hbm, mast_hbm, mom1_hbm, mom2_hbm, new_mast, new_first, new_second, full,
           grads, wres, own, got_a, got_z, sum32, sum16, own32, got_b, out16, got_c, deq, got_o,
           load_sem, send_sem, recv_sem):
    at = At()
    n_groups = len(GROUPS)
    kinds = [kind for kind, _ in GROUPS]
    sizes = [r for _, r in GROUPS]
    rows = [pl.ds(sum(sizes[:g]), r) for g, r in enumerate(sizes)]
    z_from = sum(r for kind, r in GROUPS if kind == "n")

    loads = []
    for g in range(n_groups):
        view = (slice(None),) * 4 + (rows[g],)
        loads.append(pltpu.make_async_copy(parts_hbm.at[view], grads.at[view], load_sem.at[g]))
    small = [
        pltpu.make_async_copy(src, dst, load_sem.at[n_groups + i])
        for i, (src, dst) in enumerate(
            [(wres_hbm, wres), (sres_hbm, own.at[0]), (mast_hbm, own.at[1]), (mom1_hbm, own.at[2]), (mom2_hbm, own.at[3])]
        )
    ]
    for copy in loads + small:
        copy.start()

    barrier = pltpu.get_barrier_semaphore()
    met = partners()
    for x, y, z, c in met:
        pl.semaphore_signal(barrier, inc=1, device_id=at.device(x, y, z, c), device_id_type=MESH)
    zl, c = at.pod(3)
    pl.semaphore_signal(barrier, inc=1, device_id={"outer": zl * 2 + c, "fsdp": at.f}, device_id_type=MESH)
    pl.semaphore_wait(barrier, len(met) + 1)

    send = Copies(send_sem, recv_sem)
    mine = (at.x, at.y)
    a, b, c_, d, z = {}, {}, {}, {}, {}

    def chunk(g, s, to, h):
        if kinds[g] == "n":
            return grads.at[:, h, to, 0:2, rows[g], :] if s == 0 else grads.at[to, h, :, 2:4, rows[g], :]
        if s == 0:
            return grads.at[:, at.zh, to, h:h + 1, rows[g], :]
        return grads.at[to, at.zh, :, 2 + h:3 + h, rows[g], :]

    def along(s, n):
        return at.device(x=n) if s == 0 else at.device(y=n)

    def into(g, s, k):
        return got_a.at[s, k, :, 0:(2 if kinds[g] == "n" else 1), rows[g], :]

    def ring(g):
        for s in range(2):
            i = mine[s]
            ahead, behind, across = (i + 1) % 4, (i + 3) % 4, (i + 2) % 4
            a[g, s] = [
                send(chunk(g, s, across, 0), into(g, s, 0), along(s, 1)),
                send(chunk(g, s, across, 1), into(g, s, 1), along(s, 3)),
                send(chunk(g, s, ahead, 1), into(g, s, 2), along(s, 1)),
                send(chunk(g, s, behind, 0), into(g, s, 3), along(s, 3)),
            ]

    def a1(g):
        loads[g].wait()
        ring(g)

    def z_rows(g):
        return pl.ds(sum(sizes[:g]) - z_from, sizes[g])

    def z1(g):
        loads[g].wait()
        z[g] = send(grads.at[:, 1 - at.zh, :, :, rows[g], :], got_z.at[:, :, :, z_rows(g), :], at.device(z=2))

    def z2(g):
        z[g].wait_recv()
        for y in range(NY):
            block = grads.at[y, at.zh, :, :, rows[g], :]
            block[...] = (block[...].astype(F32) + got_z[y, :, :, z_rows(g), :].astype(F32)).astype(BF)
        ring(g)

    def a2(g):
        for s in range(2):
            i = mine[s]
            for k, to, n in ((0, (i + 1) % 4, 1), (1, (i + 3) % 4, 3)):
                a[g, s][k].wait_recv()
                block = chunk(g, s, to, k)
                block[...] = (block[...].astype(F32) + into(g, s, k)[...].astype(F32)).astype(BF)
                a[g, s].append(send(block, into(g, s, 4 + k), along(s, n)))

    def a3(g):
        nz = 2 if kinds[g] == "n" else 1
        for s in range(2):
            i, j = mine[s], mine[1 - s]
            for h, (k, m) in enumerate(((4, 3), (2, 5))):
                a[g, s][k].wait_recv()
                a[g, s][m].wait_recv()
                summed = chunk(g, s, i, h)[...].astype(F32) + into(g, s, k)[...].astype(F32) + into(g, s, m)[...].astype(F32)
                if nz == 2:
                    sum32[s, :, h, :, 0:sizes[g], :] = summed
                    sum16[s, :, h, :, rows[g], :] = summed.astype(BF)
                else:
                    sum32[s, :, 0, h:h + 1, 0:sizes[g], :] = summed
                    sum16[s, :, 0, h:h + 1, rows[g], :] = summed.astype(BF)
            b[g, s] = [
                send(sum16.at[s, (j + n) % 4, 0:nz, :, rows[g], :], got_b.at[s, n - 1, 0:nz, :, rows[g], :], along(1 - s, n))
                for n in (1, 3, 2)
            ]
            own32[s, 0:nz, :, rows[g], :] = sum32[s, j, 0:nz, :, 0:sizes[g], :]

    def b1(g):
        for s in range(2):
            for copy in b[g, s]:
                copy.wait_recv()

            def second(h):
                total = own32[s, h, :, rows[g], :]
                for n in range(3):
                    total = total + got_b[s, n, h, :, rows[g], :].astype(F32)
                return total

            both = slice(2 * s, 2 * s + 2)
            if kinds[g] == "n":
                out16[both, rows[g], :] = second(1 - at.zh).astype(BF)
                deq[both, rows[g], :] = second(at.zh)
            else:
                deq[both, rows[g], :] = second(0)
        if kinds[g] == "n":
            c_[g] = send(out16.at[:, rows[g], :], got_c.at[:, rows[g], :], at.device(z=2))
        else:
            code(g, deq[:, rows[g], :])

    def c1(g):
        c_[g].wait_recv()
        code(g, deq[:, rows[g], :] + got_c[:, rows[g], :].astype(F32))

    def code(g, pod_grad):
        worker = pod_grad + wres[:, rows[g], :]
        scale = jnp.max(jnp.abs(worker), axis=-1, keepdims=True) + 1e-06
        coded = (worker / scale).astype(BF)
        deq[:, rows[g], :] = coded.astype(F32) * scale
        d[g] = []
        for j in range(1, 4):
            zl, c = at.pod(j)
            d[g].append(send(deq.at[zl * 2 + c, rows[g], :], got_o.at[j - 1, rows[g], :], {"outer": zl * 2 + c, "fsdp": at.f}))

    def d1(g):
        total = deq[at.o, rows[g], :]
        for j in range(3):
            d[g][j].wait_recv()
            total = total + got_o[j, rows[g], :]
        server = total + own[0, rows[g], :]
        scale = jnp.max(jnp.abs(server), axis=-1, keepdims=True) + 1e-06
        server_code = (server / scale).astype(BF)
        grad = server_code.astype(F32) * scale
        first = 0.9 * own[2, rows[g], :] + 0.1 * grad
        second = 0.95 * own[3, rows[g], :] + 0.05 * grad * grad
        first_hat = first / (1.0 - 0.9**STEP)
        second_hat = second / (1.0 - 0.95**STEP)
        old = own[1, rows[g], :]
        new = old - 0.01 * (first_hat / (jnp.sqrt(second_hat) + 1e-08) + 0.1 * old)
        new_mast[rows[g], :] = new
        new_first[rows[g], :] = first
        new_second[rows[g], :] = second
        full[at.y, at.zh, at.x, at.zl, at.c, rows[g], :] = new.astype(BF)

    def region(part, along_a=None, at_b=0, at_c=0):
        order, first, count = part
        here = {"x": at.x, "y": at.y, "z": at.z}
        pick = {order[1]: (here[order[1]] + at_b) % 4, order[2]: (here[order[2]] + at_c) % 4}
        if along_a == "own":
            pick[order[0]] = here[order[0]]
        if "z" in pick:
            zh, zl = pick["z"] // 2, pick["z"] % 2
        else:
            zh, zl = (slice(None) if along_a is None else slice(along_a, along_a + 1)), slice(None)
        for axis in "xy":
            if axis not in pick:
                pick[axis] = slice(None) if along_a is None else slice(2 * along_a, 2 * along_a + 2)
        return full.at[pick["y"], zh, pick["x"], zl, at.c, pl.ds(first, count), :]

    def to_axis(axis, n):
        return at.device(**{axis: n})

    sibling = at.device(c=1)
    cores, ga, gb, gc, gd = [], {}, {}, {}, {}

    def twin(part, *at_):
        piece = region(part, None, *at_)
        cores.append(send(piece, piece, sibling))

    def third(part, at_b):
        piece = region(part, None, at_b)
        gc[part, at_b] = [send(piece, piece, to_axis(part[0][2], n)) for n in (1, 3)]

    def g0(parts):
        for part in parts:
            piece = region(part, "own")
            ga[part] = [send(piece, piece, to_axis(part[0][0], n)) for n in (1, 3, 2)]

    def g1(parts):
        for part in parts:
            for copy in ga[part]:
                copy.wait_recv()
            piece = region(part)
            gb[part] = [send(piece, piece, to_axis(part[0][1], n)) for n in (1, 3, 2)]
            third(part, 0)

    def g2(parts):
        for i, at_b in enumerate((3, 1, 2)):
            for part in parts:
                gb[part][i].wait_recv()
                third(part, at_b)
        for part in parts:
            for at_b in range(4):
                twin(part, at_b)

    def g3(parts):
        for at_b in (0, 3, 1, 2):
            for part in parts:
                axis = part[0][2]
                for copy in gc[part, at_b]:
                    copy.wait_recv()
                back, front = region(part, 0, at_b, 3), region(part, 1, at_b, 1)
                gd[part, at_b] = [send(back, back, to_axis(axis, 1)), send(front, front, to_axis(axis, 3))]
                twin(part, at_b, 1)
                twin(part, at_b, 3)

    def g4(parts):
        for at_b in (0, 3, 1, 2):
            for part in parts:
                for copy in gd[part, at_b]:
                    copy.wait_recv()
                twin(part, at_b, 2)

    steps = {"a1": a1, "a2": a2, "a3": a3, "z1": z1, "z2": z2, "b": b1, "c": c1, "d": d1}
    gathers = {"g0": g0, "g1": g1, "g2": g2, "g3": g3, "g4": g4}
    for copy in small:
        copy.wait()
    for name, n in schedule():
        if name in steps:
            steps[name](n)
        else:
            gathers[name](BATCHES[n][1])
    for copy in cores:
        copy.wait_recv()
    for copy in send.started:
        copy.wait_send()


def schedule():
    order = [(t, 0, name, g) for g, times in enumerate(TIMES) for name, t in times.items()]
    order += [(t, 1, name, n) for n, times in enumerate(GATHER_TIMES) for name, t in times.items()]
    for n, (groups, _) in enumerate(BATCHES):
        order.append((max(TIMES[g]["d"] for g in groups), 1, "g0", n))
    return [(name, n) for _, _, name, n in sorted(order)]


def write_out(*refs):
    n = len(refs) // 2
    sem = refs[-1]
    copies = [pltpu.make_async_copy(refs[i], refs[n + i], sem.at[i]) for i in range(n)]
    for copy in copies:
        copy.start()
    for copy in copies:
        copy.wait()


def copies_needed():
    per_group = {"n": 2 * (6 + 3) + 1 + 3, "z": 1 + 2 * (6 + 3) + 3}
    per_part = 3 + 3 + 4 * (2 + 2 + 4)
    return sum(per_group[kind] for kind, _ in GROUPS) + per_part * sum(len(parts) for _, parts in BATCHES)


def local(partials, worker_residual, server_residual, master, first_moment, second_moment):
    grads = partials.reshape(NY, NH, NX, NL * NC, ROWS, 128)
    wres = worker_residual.reshape(NL * NC, ROWS, 128)
    flat = [v.reshape(ROWS, 128) for v in (server_residual, master, first_moment, second_moment)]
    n = copies_needed()
    hbm = pl.BlockSpec(memory_space=pltpu.HBM)
    vmem = pl.BlockSpec(memory_space=pltpu.VMEM)
    tall = max(r for _, r in GROUPS)
    z_rows = sum(r for kind, r in GROUPS if kind == "z")
    shard = pltpu.VMEM((ROWS, 128), F32)
    results = pl.pallas_call(
        kernel,
        out_shape=(shard, shard, shard, pltpu.VMEM((NY, NH, NX, NL, NC, ROWS, 128), BF)),
        in_specs=[hbm] * 6,
        out_specs=(vmem,) * 4,
        scratch_shapes=[
            pltpu.VMEM((NY, NH, NX, NL * NC, ROWS, 128), BF),
            pltpu.VMEM((NL * NC, ROWS, 128), F32),
            pltpu.VMEM((4, ROWS, 128), F32),
            pltpu.VMEM((2, 6, 4, 2, ROWS, 128), BF),
            pltpu.VMEM((NY, NX, NL * NC, max(z_rows, 16), 128), BF),
            pltpu.VMEM((2, 4, 2, 2, tall, 128), F32),
            pltpu.VMEM((2, 4, 2, 2, ROWS, 128), BF),
            pltpu.VMEM((2, 2, 2, ROWS, 128), F32),
            pltpu.VMEM((2, 3, 2, 2, ROWS, 128), BF),
            pltpu.VMEM((NL * NC, ROWS, 128), BF),
            pltpu.VMEM((NL * NC, ROWS, 128), BF),
            pltpu.VMEM((NL * NC, ROWS, 128), F32),
            pltpu.VMEM((3, ROWS, 128), F32),
            pltpu.SemaphoreType.DMA((len(GROUPS) + 5,)),
            pltpu.SemaphoreType.DMA((n,)),
            pltpu.SemaphoreType.DMA((n,)),
        ],
        compiler_params=pltpu.CompilerParams(collective_id=0, has_side_effects=True, vmem_limit_bytes=44 * 2**20),
    )(*[pltpu.with_memory_space_constraint(v, pltpu.HBM) for v in (grads, wres, *flat)])
    new_mast, new_first, new_second, full = pl.pallas_call(
        write_out,
        out_shape=[jax.ShapeDtypeStruct(v.shape, v.dtype) for v in results],
        in_specs=[pl.BlockSpec(memory_space=pl.ANY)] * 4,
        out_specs=[pl.BlockSpec(memory_space=pl.ANY)] * 4,
        scratch_shapes=[pltpu.SemaphoreType.DMA((4,))],
        compiler_params=pltpu.CompilerParams(vmem_limit_bytes=2**20),
    )(*[pltpu.with_memory_space_constraint(v, pltpu.VMEM) for v in results])
    return new_mast[None], new_first[None], new_second[None], full.reshape(NY * NH * NX * NL * NC * ROWS, 128)


def solution(mesh):
    placed = (
        P(("outer", "fsdp"), None, None),
        P("outer", "fsdp", None),
        P("fsdp", "outer", None),
        P("fsdp", "outer", None),
        P("fsdp", "outer", None),
        P("fsdp", "outer", None),
    )
    return jax.shard_map(
        local,
        mesh=mesh,
        in_specs=placed,
        out_specs=(P("fsdp", "outer", None), P("fsdp", "outer", None), P("fsdp", "outer", None), P()),
        check_vma=False,
    )
```

time: 118 us -> 94.7 us (0.80)
  Pallas kernels: 107 us -> 94 us
  local copies, waits for them, and re-layouts: 10 us -> 0 us
    pallas_call x1, Pallas kernels: 107 us -> 90.4 us  [local(): pl.pallas_call(kernel, out_shape=(shard, shard, shard, pltpu.VMEM((NY, NH...]
    unnamed x14 -> x0, local copies, waits for them, and re-layouts: 10 us -> none
    pallas_call x0 -> x1, Pallas kernels: none -> 3.56 us  [local(): pl.pallas_call(write_out, out_shape=[jax.ShapeDtypeStruct(v.shape, v.dtyp...]
where the time goes in v2:
time: 94.7 us; the launch traced here: 94.6 us
  Pallas kernels  94 us (99%)
    pallas_call x1, Pallas kernels, local(): pl.pallas_call(kernel, out_shape=(shard, shard, shard, pltpu.VMEM((NY, NH...  90.4 us
    pallas_call x1, Pallas kernels, local(): pl.pallas_call(write_out, out_shape=[jax.ShapeDtypeStruct(v.shape, v.dtyp...  3.56 us

profile of v2, /device:TPU:1, one launch (start us, length us, event | category | flops | bytes accessed | tf_op | source)
XLA Modules:
  0.0 94.6 jit_solution(17672934350490189722)
XLA Ops:
  0.6 90.4 %shard_map.93 = (f32[256,128]{1,0:T(8,128)S(1)}, f32[256,128]{1,0:T(8,128)S(1)}, f32[256,128]{1,0:T(8,128)S(1)}, bf16[4,2,4,2,2,256,128]{6,5,4,3,2,1,0:T(8,128)(2,1)S(1)}) custom-call(bf16[4,2,4,4,256,128]{5,4,3,2,1,0:T(8,128)(2,1)} %bitcast.10, f32[4,256,128]{2,1,0:T(8,128)} %bitcast.11, f32[256,128]{1,0:T(8,128)} %bitcast.12, f32[256,128]{1,0:T(8,128)} %bitcast.13, ...), custom_call_target="tpu_custom_call" | custom-call | tf_op jit(solution)/shard_map/pallas_call | solution.py:355
  91.1 3.6 %shard_map.94 = (f32[256,128]{1,0:T(8,128)}, f32[256,128]{1,0:T(8,128)}, f32[256,128]{1,0:T(8,128)}, bf16[4,2,4,2,2,256,128]{6,5,4,3,2,1,0:T(8,128)(2,1)}) custom-call(f32[256,128]{1,0:T(8,128)S(1)} %get-tuple-element.12.refs_0_, f32[256,128]{1,0:T(8,128)S(1)} %get-tuple-element.13.refs_1_, f32[256,128]{1,0:T(8,128)S(1)} %get-tuple-element.14.refs_2_, ...), custom_call_target="tpu_custom_call" | custom-call | tf_op jit(solution)/shard_map/pallas_call | solution.py:380

commit v3 on v2

--- a/solution.py
+++ b/solution.py
@@ -13,21 +13,30 @@
 NX, NY, NH, NL, NC = 4, 4, 2, 2, 2
 ROWS = 256
 
-GROUPS = (("n", 64), ("n", 64), ("n", 64), ("z", 32), ("z", 32))
+GROUPS = (("n", 48), ("n", 32), ("z", 32), ("z", 32), ("n", 96), ("z", 16))
 BATCHES = (
-    ((0, 1, 2), (("xyz", 0, 64), ("yzx", 64, 64), ("zxy", 128, 64))),
-    ((3, 4), (("xyz", 192, 16), ("yzx", 208, 16), ("zxy", 224, 32))),
+    ((0,), (("yzx", 0, 16, 0, 0),)),
+    ((0,), (("yzx", 16, 16, 0, 0),)),
+    ((0,), (("yxz", 32, 16, 0, 1),)),
+    ((1, 2), (("xzy", 48, 48, 0, 0),)),
+    ((1, 2), (("xyz", 96, 16, 0, 0),)),
+    ((3,), (("yxz", 112, 16, 0, 0),)),
+    ((3,), (("xyz", 128, 16, 0, 0),)),
+    ((4,), (("yzx", 144, 48, 0, 0), ("zxy", 192, 32, 0, 0), ("xyz", 224, 16, 1, 0))),
+    ((5,), (("xzy", 240, 16, 0, 0),)),
 )
-TIMES = (
-    {"a1": -9, "a2": 5.5, "a3": 12, "b": 18, "c": 24, "d": 29},
-    {"a1": -8, "a2": 14, "a3": 21, "b": 27, "c": 33, "d": 38},
-    {"a1": 7, "a2": 23, "a3": 30, "b": 36, "c": 42, "d": 47},
-    {"z1": -7, "z2": 14, "a2": 20, "a3": 25, "b": 31, "d": 36},
-    {"z1": -6, "z2": 24.5, "a2": 32, "a3": 37, "b": 41, "d": 45},
-)
-GATHER_TIMES = (
-    {"g1": 51, "g2": 55, "g3": 60, "g4": 64},
-    {"g1": 52, "g2": 56, "g3": 61, "g4": 65},
+ORDER = (
+    ("z1", 2), ("a1", 4), ("a1", 1), ("a2", 4), ("z1", 3), ("a2", 1), ("a1", 0), ("a3", 4),
+    ("z2", 2), ("a3", 1), ("z1", 5), ("a2", 0), ("z2", 3), ("a2", 2), ("b", 4), ("z2", 5),
+    ("b", 1), ("a3", 0), ("a2", 3), ("a3", 2), ("c", 4), ("a2", 5), ("c", 1), ("a3", 3),
+    ("b", 0), ("a3", 5), ("b", 2), ("d", 4), ("d", 1), ("g0", 7), ("b", 3), ("b", 5),
+    ("d", 2), ("c", 0), ("g0", 3), ("g0", 4), ("g1", 7), ("d", 3), ("d", 5), ("g0", 5),
+    ("g0", 6), ("g0", 8), ("d", 0), ("g1", 3), ("g0", 0), ("g0", 1), ("g0", 2), ("g1", 4),
+    ("g1", 5), ("g1", 6), ("g1", 8), ("g2", 7), ("g1", 0), ("g1", 1), ("g1", 2), ("g2", 4),
+    ("g2", 3), ("g2", 5), ("g2", 6), ("g2", 8), ("g2", 0), ("g2", 1), ("g3", 4), ("g3", 7),
+    ("g3", 5), ("g2", 2), ("g3", 0), ("g3", 6), ("g3", 3), ("g4", 4), ("g3", 1), ("g3", 8),
+    ("g4", 5), ("g4", 7), ("g3", 2), ("g4", 0), ("g4", 1), ("g4", 3), ("g4", 6), ("g4", 2),
+    ("g4", 8),
 )
 
 
@@ -80,7 +89,6 @@
     kinds = [kind for kind, _ in GROUPS]
     sizes = [r for _, r in GROUPS]
     rows = [pl.ds(sum(sizes[:g]), r) for g, r in enumerate(sizes)]
-    z_from = sum(r for kind, r in GROUPS if kind == "n")
 
     loads = []
     for g in range(n_groups):
@@ -136,7 +144,7 @@
         ring(g)
 
     def z_rows(g):
-        return pl.ds(sum(sizes[:g]) - z_from, sizes[g])
+        return pl.ds(sum(r for kind, r in GROUPS[:g] if kind == "z"), sizes[g])
 
     def z1(g):
         loads[g].wait()
@@ -234,19 +242,23 @@
         new_second[rows[g], :] = second
         full[at.y, at.zh, at.x, at.zl, at.c, rows[g], :] = new.astype(BF)
 
-    def region(part, along_a=None, at_b=0, at_c=0):
-        order, first, count = part
+    def region(part, along_a=None, at_b=None, at_c=0):
+        order, first, count = part[:3]
         here = {"x": at.x, "y": at.y, "z": at.z}
-        pick = {order[1]: (here[order[1]] + at_b) % 4, order[2]: (here[order[2]] + at_c) % 4}
+        pick = {order[2]: (here[order[2]] + at_c) % 4}
+        if at_b is not None:
+            pick[order[1]] = (here[order[1]] + at_b) % 4
         if along_a == "own":
             pick[order[0]] = here[order[0]]
+        every = slice(None)
+        half = order[0] if along_a in (0, 1) else None
         if "z" in pick:
             zh, zl = pick["z"] // 2, pick["z"] % 2
         else:
-            zh, zl = (slice(None) if along_a is None else slice(along_a, along_a + 1)), slice(None)
+            zh, zl = (slice(along_a, along_a + 1) if half == "z" else every), every
         for axis in "xy":
             if axis not in pick:
-                pick[axis] = slice(None) if along_a is None else slice(2 * along_a, 2 * along_a + 2)
+                pick[axis] = slice(2 * along_a, 2 * along_a + 2) if half == axis else every
         return full.at[pick["y"], zh, pick["x"], zl, at.c, pl.ds(first, count), :]
 
     def to_axis(axis, n):
@@ -262,43 +274,58 @@
     def third(part, at_b):
         piece = region(part, None, at_b)
         gc[part, at_b] = [send(piece, piece, to_axis(part[0][2], n)) for n in (1, 3)]
+        if part[4]:
+            gd[part, at_b] = [send(piece, piece, to_axis(part[0][2], 2))]
+
+    def blocks(part):
+        return (0, 3, 1, 2) if part[3] else (None,)
 
     def g0(parts):
         for part in parts:
-            piece = region(part, "own")
+            piece = region(part, "own", 0)
             ga[part] = [send(piece, piece, to_axis(part[0][0], n)) for n in (1, 3, 2)]
 
     def g1(parts):
         for part in parts:
             for copy in ga[part]:
                 copy.wait_recv()
-            piece = region(part)
+            piece = region(part, None, 0)
             gb[part] = [send(piece, piece, to_axis(part[0][1], n)) for n in (1, 3, 2)]
-            third(part, 0)
+            if part[3]:
+                third(part, 0)
 
     def g2(parts):
         for i, at_b in enumerate((3, 1, 2)):
             for part in parts:
                 gb[part][i].wait_recv()
-                third(part, at_b)
+                if part[3]:
+                    third(part, at_b)
+                elif i == 2:
+                    third(part, None)
         for part in parts:
-            for at_b in range(4):
+            for at_b in blocks(part):
                 twin(part, at_b)
 
     def g3(parts):
-        for at_b in (0, 3, 1, 2):
+        for i in range(4):
             for part in parts:
-                axis = part[0][2]
+                if i >= len(blocks(part)):
+                    continue
+                at_b, axis = blocks(part)[i], part[0][2]
                 for copy in gc[part, at_b]:
                     copy.wait_recv()
-                back, front = region(part, 0, at_b, 3), region(part, 1, at_b, 1)
-                gd[part, at_b] = [send(back, back, to_axis(axis, 1)), send(front, front, to_axis(axis, 3))]
+                if not part[4]:
+                    back, front = region(part, 0, at_b, 3), region(part, 1, at_b, 1)
+                    gd[part, at_b] = [send(back, back, to_axis(axis, 1)), send(front, front, to_axis(axis, 3))]
                 twin(part, at_b, 1)
                 twin(part, at_b, 3)
 
     def g4(parts):
-        for at_b in (0, 3, 1, 2):
+        for i in range(4):
             for part in parts:
+                if i >= len(blocks(part)):
+                    continue
+                at_b = blocks(part)[i]
                 for copy in gd[part, at_b]:
                     copy.wait_recv()
                 twin(part, at_b, 2)
@@ -307,7 +334,7 @@
     gathers = {"g0": g0, "g1": g1, "g2": g2, "g3": g3, "g4": g4}
     for copy in small:
         copy.wait()
-    for name, n in schedule():
+    for name, n in ORDER:
         if name in steps:
             steps[name](n)
         else:
@@ -318,18 +345,12 @@
         copy.wait_send()
 
 
-def schedule():
-    order = [(t, 0, name, g) for g, times in enumerate(TIMES) for name, t in times.items()]
-    order += [(t, 1, name, n) for n, times in enumerate(GATHER_TIMES) for name, t in times.items()]
-    for n, (groups, _) in enumerate(BATCHES):
-        order.append((max(TIMES[g]["d"] for g in groups), 1, "g0", n))
-    return [(name, n) for _, _, name, n in sorted(order)]
-
-
 def write_out(*refs):
     n = len(refs) // 2
     sem = refs[-1]
-    copies = [pltpu.make_async_copy(refs[i], refs[n + i], sem.at[i]) for i in range(n)]
+    pairs = [(refs[i], refs[n + i]) for i in range(n - 1)]
+    pairs += [(refs[n - 1].at[y, h], refs[2 * n - 1].at[y, h]) for y in range(NY) for h in range(NH)]
+    copies = [pltpu.make_async_copy(src, dst, sem.at[i]) for i, (src, dst) in enumerate(pairs)]
     for copy in copies:
         copy.start()
     for copy in copies:
@@ -338,8 +359,12 @@
 
 def copies_needed():
     per_group = {"n": 2 * (6 + 3) + 1 + 3, "z": 1 + 2 * (6 + 3) + 3}
-    per_part = 3 + 3 + 4 * (2 + 2 + 4)
-    return sum(per_group[kind] for kind, _ in GROUPS) + per_part * sum(len(parts) for _, parts in BATCHES)
+    per_part = [
+        6 + (4 if passed else 1) * ((3 if direct else 4) + 4)
+        for _, parts in BATCHES
+        for *_, passed, direct in parts
+    ]
+    return sum(per_group[kind] for kind, _ in GROUPS) + sum(per_part)
 
 
 def local(partials, worker_residual, server_residual, master, first_moment, second_moment):
@@ -382,7 +407,7 @@
         out_shape=[jax.ShapeDtypeStruct(v.shape, v.dtype) for v in results],
         in_specs=[pl.BlockSpec(memory_space=pl.ANY)] * 4,
         out_specs=[pl.BlockSpec(memory_space=pl.ANY)] * 4,
-        scratch_shapes=[pltpu.SemaphoreType.DMA((4,))],
+        scratch_shapes=[pltpu.SemaphoreType.DMA((3 + NY * NH,))],
         compiler_params=pltpu.CompilerParams(vmem_limit_bytes=2**20),
     )(*[pltpu.with_memory_space_constraint(v, pltpu.VMEM) for v in results])
     return new_mast[None], new_first[None], new_second[None], full.reshape(NY * NH * NX * NL * NC * ROWS, 128)

time: 94.7 us -> 86.4 us (0.912)
  Pallas kernels: 94 us -> 85.6 us
    pallas_call x1, Pallas kernels: 90.4 us -> 82.1 us  [local(): pl.pallas_call(kernel, out_shape=(shard, shard, shard, pltpu.VMEM((NY, NH...]
where the time goes in v3:
time: 86.4 us; the launch traced here: 86.3 us
  Pallas kernels  85.6 us (99%)
    pallas_call x1, Pallas kernels, local(): pl.pallas_call(kernel, out_shape=(shard, shard, shard, pltpu.VMEM((NY, NH...  82.1 us
    pallas_call x1, Pallas kernels, local(): pl.pallas_call(write_out, out_shape=[jax.ShapeDtypeStruct(v.shape, v.dtyp...  3.52 us

profile of v3, /device:TPU:1, one launch (start us, length us, event | category | flops | bytes accessed | tf_op | source)
XLA Modules:
  0.0 86.3 jit_solution(11259119945421036314)
XLA Ops:
  0.6 82.1 %shard_map.93 = (f32[256,128]{1,0:T(8,128)S(1)}, f32[256,128]{1,0:T(8,128)S(1)}, f32[256,128]{1,0:T(8,128)S(1)}, bf16[4,2,4,2,2,256,128]{6,5,4,3,2,1,0:T(8,128)(2,1)S(1)}) custom-call(bf16[4,2,4,4,256,128]{5,4,3,2,1,0:T(8,128)(2,1)} %bitcast.10, f32[4,256,128]{2,1,0:T(8,128)} %bitcast.11, f32[256,128]{1,0:T(8,128)} %bitcast.12, f32[256,128]{1,0:T(8,128)} %bitcast.13, ...), custom_call_target="tpu_custom_call" | custom-call | tf_op jit(solution)/shard_map/pallas_call | solution.py:380
  82.7 3.5 %shard_map.94 = (f32[256,128]{1,0:T(8,128)}, f32[256,128]{1,0:T(8,128)}, f32[256,128]{1,0:T(8,128)}, bf16[4,2,4,2,2,256,128]{6,5,4,3,2,1,0:T(8,128)(2,1)}) custom-call(f32[256,128]{1,0:T(8,128)S(1)} %get-tuple-element.12.refs_0_, f32[256,128]{1,0:T(8,128)S(1)} %get-tuple-element.13.refs_1_, f32[256,128]{1,0:T(8,128)S(1)} %get-tuple-element.14.refs_2_, ...), custom_call_target="tpu_custom_call" | custom-call | tf_op jit(solution)/shard_map/pallas_call | solution.py:405

commit v4 on v3

--- a/solution.py
+++ b/solution.py
@@ -25,6 +25,7 @@
     ((4,), (("yzx", 144, 48, 0, 0), ("zxy", 192, 32, 0, 0), ("xyz", 224, 16, 1, 0))),
     ((5,), (("xzy", 240, 16, 0, 0),)),
 )
+LAG = 12
 ORDER = (
     ("z1", 2), ("a1", 4), ("a1", 1), ("a2", 4), ("z1", 3), ("a2", 1), ("a1", 0), ("a3", 4),
     ("z2", 2), ("a3", 1), ("z1", 5), ("a2", 0), ("z2", 3), ("a2", 2), ("b", 4), ("z2", 5),
@@ -334,14 +335,22 @@
     gathers = {"g0": g0, "g1": g1, "g2": g2, "g3": g3, "g4": g4}
     for copy in small:
         copy.wait()
-    for name, n in ORDER:
+    ended, n_cores = [], []
+    for i, (name, n) in enumerate(ORDER):
         if name in steps:
             steps[name](n)
         else:
             gathers[name](BATCHES[n][1])
-    for copy in cores:
+        ended.append(len(send.started))
+        n_cores.append(len(cores))
+        if i >= LAG:
+            for copy in send.started[ended[i - LAG - 1] if i > LAG else 0:ended[i - LAG]]:
+                copy.wait_send()
+            for copy in cores[n_cores[i - LAG - 1] if i > LAG else 0:n_cores[i - LAG]]:
+                copy.wait_recv()
+    for copy in cores[n_cores[-LAG - 1]:]:
         copy.wait_recv()
-    for copy in send.started:
+    for copy in send.started[ended[-LAG - 1]:]:
         copy.wait_send()
 
 

time: 86.4 us -> 85.9 us (level)
  no operation moved by 1% of the time
where the time goes in v4:
time: 85.9 us; the launch traced here: 85.8 us
  Pallas kernels  85.2 us (99%)
    pallas_call x1, Pallas kernels, local(): pl.pallas_call(kernel, out_shape=(shard, shard, shard, pltpu.VMEM((NY, NH...  81.7 us
    pallas_call x1, Pallas kernels, local(): pl.pallas_call(write_out, out_shape=[jax.ShapeDtypeStruct(v.shape, v.dtyp...  3.52 us

profile of v4, /device:TPU:1, one launch (start us, length us, event | category | flops | bytes accessed | tf_op | source)
XLA Modules:
  0.0 85.8 jit_solution(5206001628334076308)
XLA Ops:
  0.6 81.7 %shard_map.93 = (f32[256,128]{1,0:T(8,128)S(1)}, f32[256,128]{1,0:T(8,128)S(1)}, f32[256,128]{1,0:T(8,128)S(1)}, bf16[4,2,4,2,2,256,128]{6,5,4,3,2,1,0:T(8,128)(2,1)S(1)}) custom-call(bf16[4,2,4,4,256,128]{5,4,3,2,1,0:T(8,128)(2,1)} %bitcast.10, f32[4,256,128]{2,1,0:T(8,128)} %bitcast.11, f32[256,128]{1,0:T(8,128)} %bitcast.12, f32[256,128]{1,0:T(8,128)} %bitcast.13, ...), custom_call_target="tpu_custom_call" | custom-call | tf_op jit(solution)/shard_map/pallas_call | solution.py:389
  82.3 3.5 %shard_map.94 = (f32[256,128]{1,0:T(8,128)}, f32[256,128]{1,0:T(8,128)}, f32[256,128]{1,0:T(8,128)}, bf16[4,2,4,2,2,256,128]{6,5,4,3,2,1,0:T(8,128)(2,1)}) custom-call(f32[256,128]{1,0:T(8,128)S(1)} %get-tuple-element.12.refs_0_, f32[256,128]{1,0:T(8,128)S(1)} %get-tuple-element.13.refs_1_, f32[256,128]{1,0:T(8,128)S(1)} %get-tuple-element.14.refs_2_, ...), custom_call_target="tpu_custom_call" | custom-call | tf_op jit(solution)/shard_map/pallas_call | solution.py:414
